TPU v7x, 32 devices: a whole 2x2x4 slice. The times are simulated.
32 devices in a mesh: world: 2 (over x), gx: 16 (over z, y, core).
Axes of the slice: x: 2, y: 2, z: 4, core: 2. Of those that a mesh axis runs over, the one named last changes fastest.
Arguments:
- field: float32 [32, 256, 64, 128], P(None, ('world', 'gx')), parts along dimension 1, may hold values from -12 to 12
- occupancy: int32 [256, 64, 128], P(('world', 'gx')), parts along dimension 0, may hold values 0 or 1
- duals: float32 [64, 32], P('world'), parts along dimension 0, may hold values from -4 to 4
Outputs:
- field_out: float32 [32, 256, 64, 128], P(None, ('world', 'gx')), parts along dimension 1
- duals_out: float32 [64, 32], P('world'), parts along dimension 0
There are 2 independent parts, one for each index of `world`. A program takes and returns all parts, laid end to end along the dimension named above; each array names one. Nothing has to cross between parts.
All inputs are finite; a program needn't handle non-finite values. No bound on the sum of `occupancy` on one device may be relied on, other than what follows from the above.
Results may differ from a plain program's by a relative error of at most 0.0001.
Values sent between devices are 32-bit elements; how exact they have to be, the bound alone decides.
A program may use at most 128 MiB of HBM per device.

v0:
```python
import functools

import jax
import jax.numpy as jnp
from jax import lax
from jax.experimental import pallas as pl
from jax.experimental.pallas import tpu as pltpu
from jax.sharding import PartitionSpec as P

MESH = pl.DeviceIdType.MESH
HI = lax.Precision.HIGHEST
S8 = 8
F32 = jnp.float32
BF16 = jnp.bfloat16


def iota(shape, dim):
    return lax.broadcasted_iota(jnp.int32, shape, dim)


def dot_nt(a, b, precision=None):
    return lax.dot_general(a, b, (((1,), (1,)), ((), ())), precision=precision, preferred_element_type=F32)


def dot_nn(a, b, precision=None):
    return lax.dot_general(a, b, (((1,), (0,)), ((), ())), precision=precision, preferred_element_type=F32)


def split(x):
    high = x.astype(BF16)
    return high, (x - high.astype(F32)).astype(BF16)


def kernel(n, field, occ, duals, out, duals_out, u, v0, v1, parts, mask, keep, acc, mix, shift,
           gsend, gbuf, in_sem, out_sem, h_send, h_recv, m_send, m_recv, g_send, g_recv):
    me = lax.axis_index("gx")
    rows, channels, depth, across = u.shape
    wide = channels * S8
    groups = depth // S8
    count = n * rows * depth * across
    last = rows + 1

    barrier = pltpu.get_barrier_semaphore()

    def greet(d, c):
        pl.semaphore_signal(barrier, inc=1, device_id={"gx": lax.rem(me + d, n)}, device_id_type=MESH)
        return c

    lax.fori_loop(1, n, greet, 0)

    def fetch(x):
        return pltpu.make_async_copy(field.at[:, x], u.at[x], in_sem.at[x])

    fetch(0).start()
    fetch(rows - 1).start()
    for x in range(1, rows - 1):
        fetch(x).start()

    for x in range(rows):
        mask[x + 1] = occ[x].astype(F32)

    @pl.when(me == 0)
    def _():
        mask[0] = jnp.zeros((depth, across), F32)
        v0[0] = jnp.zeros((channels, depth, across), F32)
        v1[0] = jnp.zeros((channels, depth, across), F32)

    @pl.when(me == n - 1)
    def _():
        mask[last] = jnp.zeros((depth, across), F32)
        v0[last] = jnp.zeros((channels, depth, across), F32)
        v1[last] = jnp.zeros((channels, depth, across), F32)

    def to_left(src, dst, send, recv):
        return pltpu.make_async_remote_copy(src_ref=src, dst_ref=dst, send_sem=send, recv_sem=recv,
                                            device_id={"gx": me - 1}, device_id_type=MESH)

    def to_right(src, dst, send, recv):
        return pltpu.make_async_remote_copy(src_ref=src, dst_ref=dst, send_sem=send, recv_sem=recv,
                                            device_id={"gx": me + 1}, device_id_type=MESH)

    mask_l = to_left(mask.at[1], mask.at[last], m_send.at[0], m_recv.at[0])
    mask_r = to_right(mask.at[rows], mask.at[0], m_send.at[1], m_recv.at[1])
    u_l = to_left(u.at[0], v0.at[last], h_send.at[0], h_recv.at[0])
    u_r = to_right(u.at[rows - 1], v0.at[0], h_send.at[1], h_recv.at[1])
    w_l = to_left(v1.at[1], v1.at[last], h_send.at[2], h_recv.at[2])
    w_r = to_right(v1.at[rows], v1.at[0], h_send.at[3], h_recv.at[3])

    pl.semaphore_wait(barrier, n - 1)

    @pl.when(me > 0)
    def _():
        mask_l.start()

    @pl.when(me < n - 1)
    def _():
        mask_r.start()

    fetch(0).wait()

    @pl.when(me > 0)
    def _():
        u_l.start()

    fetch(rows - 1).wait()

    @pl.when(me < n - 1)
    def _():
        u_r.start()

    lane_shift = (jnp.abs(iota((across, across), 0) - iota((across, across), 1)) == 1).astype(F32).astype(BF16)
    shift[0:across] = lane_shift
    shift[across:2 * across] = lane_shift

    def spread(columns):
        return (iota((wide, columns), 0) // S8 == iota((wide, columns), 1)).astype(F32)

    def same_slot():
        return iota((wide, wide), 0) % S8 == iota((wide, wide), 1) % S8

    def store_parts(x, g, v):
        high, low = split(v.reshape(wide, across))
        parts[x, 0:wide, g * across:(g + 1) * across] = high
        parts[x, wide:2 * wide, g * across:(g + 1) * across] = low

    def add_gram(x):
        acc[...] += dot_nt(parts[x, 0:wide, :], parts[x])

    acc[...] = jnp.zeros_like(acc)

    def load_row(x, c):
        for g in range(groups):
            z = slice(g * S8, (g + 1) * S8)
            v = mask[x + 1, z][None] * u[x, :, z, :]
            v0[x + 1, :, z, :] = v
            store_parts(x, g, v)
        add_gram(x)
        return c

    def fetch_row(x, c):
        fetch(x).wait()
        return load_row(x, c)

    lax.fori_loop(1, rows - 1, fetch_row, 0)
    load_row(0, 0)
    load_row(rows - 1, 0)

    def gram_copy(r, d):
        return pltpu.make_async_remote_copy(
            src_ref=gsend.at[r], dst_ref=gbuf.at[r, d], send_sem=g_send.at[r, d], recv_sem=g_recv.at[r, d],
            device_id={"gx": lax.rem(me + d, n)}, device_id_type=MESH)

    def gram_start(r):
        same = same_slot()
        e_t = (iota((channels, wide), 0) == iota((channels, wide), 1) // S8).astype(F32)
        e = spread(across)
        hh = dot_nn(dot_nn(e_t, jnp.where(same, acc[:, 0:wide], 0.0), HI), e, HI)
        hl = dot_nn(dot_nn(e_t, jnp.where(same, acc[:, wide:2 * wide], 0.0), HI), e, HI)
        eye = (iota((channels, channels), 0) == iota((channels, channels), 1)).astype(F32)
        eye_wide = (iota((channels, across), 0) == iota((channels, across), 1)).astype(F32)
        lh = lax.dot_general(hl[:, 0:channels], eye_wide, (((0,), (0,)), ((), ())), precision=HI,
                             preferred_element_type=F32)
        gsend[r] = hh + hl + lh
        lax.fori_loop(1, n, lambda d, c: (gram_copy(r, d).start(), c)[1], 0)

    def gram_end(r):
        def body(d, c):
            gram_copy(r, d).wait()
            return c

        lax.fori_loop(1, n, body, 0)

        def add(d, total):
            return total + gbuf[r, d]

        total = lax.fori_loop(1, n, add, gsend[r])
        return total[:, 0:channels] / count

    def mixing(g, beta):
        row, col = iota((channels, channels), 0), iota((channels, channels), 1)
        low = row >= col
        excess = g - (row == col).astype(F32)
        q = jnp.where(low, beta + 1.0 * excess, 0.0)
        e = spread(channels)
        big = jnp.where(same_slot(), -dot_nt(dot_nn(e, q, HI), e, HI), 0.0)
        high, rest = split(big)
        mix[:, 0:wide] = high
        mix[:, wide:2 * wide] = high
        mix[:, 2 * wide:3 * wide] = rest
        return beta + 0.5 * jnp.where(low, excess, 0.0)

    sub = iota((1, S8, across), 1)

    def advance_row(v, x, write):
        zero = jnp.zeros((channels, S8, across), F32)
        pairs = 2
        for g0 in range(0, groups, pairs):
            cols = slice(g0 * across, (g0 + pairs) * across)
            mixed = dot_nn(mix[:, 0:2 * wide], parts[x, :, cols]) + dot_nn(mix[:, 2 * wide:], parts[x, 0:wide, cols])
            sides = []
            for g in range(g0, g0 + pairs):
                own = slice(g * across, (g + 1) * across)
                sides.append(dot_nn(parts[x, 0:wide, own], shift[0:across])
                             + dot_nn(parts[x, wide:2 * wide, own], shift[across:2 * across]))
            for i, g in enumerate(range(g0, g0 + pairs)):
                z = slice(g * S8, (g + 1) * S8)
                core = v[x + 1, :, z, :]
                before = v[x + 1, :, (g - 1) * S8:g * S8, :] if g > 0 else zero
                after = v[x + 1, :, (g + 1) * S8:(g + 2) * S8, :] if g < groups - 1 else zero
                up = pltpu.roll(jnp.where(sub == S8 - 1, before, core), 1, 1)
                down = pltpu.roll(jnp.where(sub == 0, after, core), S8 - 1, 1)
                total = (mixed[:, i * across:(i + 1) * across] + sides[i]).reshape(channels, S8, across)
                total = total + up + down + v[x, :, z, :] + v[x + 2, :, z, :]
                new = keep[x, z][None] * core + (0.1 * mask[x + 1, z])[None] * total
                write(x, g, z, new)

    def write_first(x, g, z, new):
        v1[x + 1, :, z, :] = new
        store_parts(x, g, new)

    def write_last(x, g, z, new):
        u[x, :, z, :] = jnp.where(mask[x + 1, z][None] > 0.5, new, u[x, :, z, :])

    gram_start(0)

    @pl.when(me > 0)
    def _():
        mask_r.wait_recv()

    @pl.when(me < n - 1)
    def _():
        mask_l.wait_recv()

    zi, yi = iota((depth, across), 0), iota((depth, across), 1)

    def weigh(x, c):
        m = mask[x + 1]
        near = mask[x] + mask[x + 2]
        near = near + jnp.where(yi == 0, 0.0, pltpu.roll(m, 1, 1))
        near = near + jnp.where(yi == across - 1, 0.0, pltpu.roll(m, across - 1, 1))
        near = near + jnp.where(zi == 0, 0.0, pltpu.roll(m, 1, 0))
        near = near + jnp.where(zi == depth - 1, 0.0, pltpu.roll(m, depth - 1, 0))
        keep[x] = m * (1.0 - 0.1 * near)
        return c

    lax.fori_loop(0, rows, weigh, 0)

    beta = mixing(gram_end(0), duals[...])
    acc[...] = jnp.zeros_like(acc)

    def first(x, c):
        advance_row(v0, x, write_first)
        add_gram(x)
        return c

    lax.fori_loop(1, rows - 1, first, 0)

    @pl.when(me > 0)
    def _():
        u_r.wait_recv()
        v0[0] = v0[0] * mask[0][None]

    first(0, 0)

    @pl.when(me > 0)
    def _():
        w_l.start()

    @pl.when(me < n - 1)
    def _():
        u_l.wait_recv()
        v0[last] = v0[last] * mask[last][None]

    first(rows - 1, 0)

    @pl.when(me < n - 1)
    def _():
        w_r.start()

    gram_start(1)
    beta = mixing(gram_end(1), beta)
    duals_out[...] = beta

    def store(x):
        return pltpu.make_async_copy(u.at[x], out.at[:, x], out_sem.at[x])

    def second(x, c):
        advance_row(v1, x, write_last)
        store(x).start()
        return c

    lax.fori_loop(1, rows - 1, second, 0)

    @pl.when(me > 0)
    def _():
        mask_l.wait_send()
        u_l.wait_send()
        w_r.wait_recv()

    @pl.when(me < n - 1)
    def _():
        mask_r.wait_send()
        u_r.wait_send()
        w_l.wait_recv()

    second(0, 0)
    second(rows - 1, 0)

    @pl.when(me > 0)
    def _():
        w_l.wait_send()

    @pl.when(me < n - 1)
    def _():
        w_r.wait_send()

    lax.fori_loop(0, rows, lambda x, c: (store(x).wait(), c)[1], 0)


def per_device(field, occupancy, duals):
    channels, rows, depth, across = field.shape
    n = lax.axis_size("gx")
    wide = channels * S8
    vmem = pl.BlockSpec(memory_space=pltpu.VMEM)
    dma = pltpu.SemaphoreType.DMA
    return pl.pallas_call(
        functools.partial(kernel, n),
        out_shape=(jax.ShapeDtypeStruct(field.shape, F32), jax.ShapeDtypeStruct(duals.shape, F32)),
        in_specs=[pl.BlockSpec(memory_space=pl.ANY), vmem, vmem],
        out_specs=(pl.BlockSpec(memory_space=pl.ANY), vmem),
        scratch_shapes=[
            pltpu.VMEM((rows, channels, depth, across), F32),
            pltpu.VMEM((rows + 2, channels, depth, across), F32),
            pltpu.VMEM((rows + 2, channels, depth, across), F32),
            pltpu.VMEM((rows, 2 * wide, depth // S8 * across), BF16),
            pltpu.VMEM((rows + 2, depth, across), F32),
            pltpu.VMEM((rows, depth, across), F32),
            pltpu.VMEM((wide, 2 * wide), F32),
            pltpu.VMEM((wide, 3 * wide), BF16),
            pltpu.VMEM((2 * across, across), BF16),
            pltpu.VMEM((2, channels, across), F32),
            pltpu.VMEM((2, n, channels, across), F32),
            dma((rows,)), dma((rows,)), dma((4,)), dma((4,)), dma((2,)), dma((2,)), dma((2, n)), dma((2, n)),
        ],
        compiler_params=pltpu.CompilerParams(
            collective_id=0, has_side_effects=True, vmem_limit_bytes=56 * 1024 * 1024),
    )(field, occupancy, duals)


def solution(mesh):
    placed = (
        P(None, ("world", "gx"), None, None),
        P(("world", "gx"), None, None),
        P("world", None),
    )
    return jax.shard_map(
        per_device,
        mesh=mesh,
        in_specs=placed,
        out_specs=(P(None, ("world", "gx"), None, None), P("world", None)),
        check_vma=False,
    )
```

profile of v0, /device:TPU:11, one launch (start us, length us, event | category | flops | bytes accessed | tf_op | source)
XLA Modules:
  0.0 92.9 jit_solution(2826548036121673415)
XLA Ops:
  0.6 83.1 %shard_map.50 = (f32[32,8,64,128]{3,2,1,0:T(8,128)}, f32[32,32]{1,0:T(8,128)}) custom-call(f32[32,8,64,128]{3,2,1,0:T(8,128)} %field.1, s32[8,64,128]{2,1,0:T(8,128)} %occ.1, f32[32,32]{1,0:T(8,128)} %duals.1), custom_call_target="tpu_custom_call" | custom-call | tf_op jit(solution)/shard_map/pallas_call | solution.py:326
  83.8 0.0 copy-start
  83.8 8.4 %copy.7 = f32[32,8,64,128]{3,2,1,0:T(8,128)} copy(f32[32,8,64,128]{3,2,1,0:T(8,128)} %get-tuple-element.4) | data formatting | bytes 16777216
  92.2 0.0 copy-done
  92.2 0.6 copy.8
Async XLA Ops:
  83.8 8.5 %copy-start = (f32[32,32]{1,0:T(8,128)S(1)}, f32[32,32]{1,0:T(8,128)}, u32[]{:S(2)}) copy-start(f32[32,32]{1,0:T(8,128)} %get-tuple-element.5) | copy-start | bytes 12292
where the time goes:
time: 93.7 us; the launch traced here: 92.9 us
  Pallas kernels  83.1 us (89%)
  local copies, waits for them, and re-layouts  9.06 us (10%)
    pallas_call x1, Pallas kernels, per_device(): pl.pallas_call(functools.partial(kernel, n), out_shape=(jax.ShapeDtypeStr...  83.1 us
    unnamed x4, local copies, waits for them, and re-layouts  9.06 us

commit v1 on v0

--- a/solution.py
+++ b/solution.py
@@ -81,10 +81,12 @@
 
     mask_l = to_left(mask.at[1], mask.at[last], m_send.at[0], m_recv.at[0])
     mask_r = to_right(mask.at[rows], mask.at[0], m_send.at[1], m_recv.at[1])
-    u_l = to_left(u.at[0], v0.at[last], h_send.at[0], h_recv.at[0])
-    u_r = to_right(u.at[rows - 1], v0.at[0], h_send.at[1], h_recv.at[1])
-    w_l = to_left(v1.at[1], v1.at[last], h_send.at[2], h_recv.at[2])
-    w_r = to_right(v1.at[rows], v1.at[0], h_send.at[3], h_recv.at[3])
+    cut = channels * 3 // 8
+    pieces = (pl.ds(0, cut), pl.ds(cut, channels - cut))
+    u_l = [to_left(u.at[0, p], v0.at[last, p], h_send.at[i], h_recv.at[i]) for i, p in enumerate(pieces)]
+    u_r = [to_right(u.at[rows - 1, p], v0.at[0, p], h_send.at[2 + i], h_recv.at[2 + i]) for i, p in enumerate(pieces)]
+    w_l = to_left(v1.at[1], v1.at[last], h_send.at[4], h_recv.at[4])
+    w_r = to_right(v1.at[rows], v1.at[0], h_send.at[5], h_recv.at[5])
 
     pl.semaphore_wait(barrier, n - 1)
 
@@ -100,13 +102,13 @@
 
     @pl.when(me > 0)
     def _():
-        u_l.start()
+        u_l[0].start()
 
     fetch(rows - 1).wait()
 
     @pl.when(me < n - 1)
     def _():
-        u_r.start()
+        u_r[0].start()
 
     lane_shift = (jnp.abs(iota((across, across), 0) - iota((across, across), 1)) == 1).astype(F32).astype(BF16)
     shift[0:across] = lane_shift
@@ -160,7 +162,11 @@
         eye_wide = (iota((channels, across), 0) == iota((channels, across), 1)).astype(F32)
         lh = lax.dot_general(hl[:, 0:channels], eye_wide, (((0,), (0,)), ((), ())), precision=HI,
                              preferred_element_type=F32)
-        gsend[r] = hh + hl + lh
+        whole = hh + hl + lh
+        packed = whole[0:S8]
+        for b in range(1, channels // S8):
+            packed = packed + pltpu.roll(whole[b * S8:(b + 1) * S8], channels * b, 1)
+        gsend[r] = packed
         lax.fori_loop(1, n, lambda d, c: (gram_copy(r, d).start(), c)[1], 0)
 
     def gram_end(r):
@@ -174,7 +180,10 @@
             return total + gbuf[r, d]
 
         total = lax.fori_loop(1, n, add, gsend[r])
-        return total[:, 0:channels] / count
+        blocks = [total[:, 0:channels]]
+        for b in range(1, channels // S8):
+            blocks.append(pltpu.roll(total, across - channels * b, 1)[:, 0:channels])
+        return jnp.concatenate(blocks, axis=0) / count
 
     def mixing(g, beta):
         row, col = iota((channels, channels), 0), iota((channels, channels), 1)
@@ -225,6 +234,14 @@
 
     @pl.when(me > 0)
     def _():
+        u_l[1].start()
+
+    @pl.when(me < n - 1)
+    def _():
+        u_r[1].start()
+
+    @pl.when(me > 0)
+    def _():
         mask_r.wait_recv()
 
     @pl.when(me < n - 1)
@@ -257,27 +274,30 @@
 
     @pl.when(me > 0)
     def _():
-        u_r.wait_recv()
+        u_r[0].wait_recv()
+        u_r[1].wait_recv()
         v0[0] = v0[0] * mask[0][None]
 
     first(0, 0)
 
+    @pl.when(me < n - 1)
+    def _():
+        u_l[0].wait_recv()
+        u_l[1].wait_recv()
+        v0[last] = v0[last] * mask[last][None]
+
+    first(rows - 1, 0)
+
+    gram_start(1)
+
     @pl.when(me > 0)
     def _():
         w_l.start()
 
     @pl.when(me < n - 1)
     def _():
-        u_l.wait_recv()
-        v0[last] = v0[last] * mask[last][None]
-
-    first(rows - 1, 0)
-
-    @pl.when(me < n - 1)
-    def _():
         w_r.start()
 
-    gram_start(1)
     beta = mixing(gram_end(1), beta)
     duals_out[...] = beta
 
@@ -294,13 +314,15 @@
     @pl.when(me > 0)
     def _():
         mask_l.wait_send()
-        u_l.wait_send()
+        u_l[0].wait_send()
+        u_l[1].wait_send()
         w_r.wait_recv()
 
     @pl.when(me < n - 1)
     def _():
         mask_r.wait_send()
-        u_r.wait_send()
+        u_r[0].wait_send()
+        u_r[1].wait_send()
         w_l.wait_recv()
 
     second(0, 0)
@@ -338,9 +360,9 @@
             pltpu.VMEM((wide, 2 * wide), F32),
             pltpu.VMEM((wide, 3 * wide), BF16),
             pltpu.VMEM((2 * across, across), BF16),
-            pltpu.VMEM((2, channels, across), F32),
-            pltpu.VMEM((2, n, channels, across), F32),
-            dma((rows,)), dma((rows,)), dma((4,)), dma((4,)), dma((2,)), dma((2,)), dma((2, n)), dma((2, n)),
+            pltpu.VMEM((2, S8, across), F32),
+            pltpu.VMEM((2, n, S8, across), F32),
+            dma((rows,)), dma((rows,)), dma((6,)), dma((6,)), dma((2,)), dma((2,)), dma((2, n)), dma((2, n)),
         ],
         compiler_params=pltpu.CompilerParams(
             collective_id=0, has_side_effects=True, vmem_limit_bytes=56 * 1024 * 1024),

time: 93.7 us -> 77 us (0.82)
  Pallas kernels: 83.1 us -> 67.1 us
    pallas_call x1, Pallas kernels: 83.1 us -> 67.1 us  [per_device(): pl.pallas_call(functools.partial(kernel, n), out_shape=(jax.ShapeDtypeStr...]
where the time goes in v1:
time: 77 us; the launch traced here: 76.8 us
  Pallas kernels  67.1 us (87%)
  local copies, waits for them, and re-layouts  9.06 us (12%)
    pallas_call x1, Pallas kernels, per_device(): pl.pallas_call(functools.partial(kernel, n), out_shape=(jax.ShapeDtypeStr...  67.1 us
    unnamed x4, local copies, waits for them, and re-layouts  9.06 us

profile of v1, /device:TPU:11, one launch (start us, length us, event | category | flops | bytes accessed | tf_op | source)
XLA Modules:
  0.0 76.8 jit_solution(11341552805695196780)
XLA Ops:
  0.6 67.1 %shard_map.50 = (f32[32,8,64,128]{3,2,1,0:T(8,128)}, f32[32,32]{1,0:T(8,128)}) custom-call(f32[32,8,64,128]{3,2,1,0:T(8,128)} %field.1, s32[8,64,128]{2,1,0:T(8,128)} %occ.1, f32[32,32]{1,0:T(8,128)} %duals.1), custom_call_target="tpu_custom_call" | custom-call | tf_op jit(solution)/shard_map/pallas_call | solution.py:348
  67.7 0.0 copy-start
  67.8 8.4 %copy.7 = f32[32,8,64,128]{3,2,1,0:T(8,128)} copy(f32[32,8,64,128]{3,2,1,0:T(8,128)} %get-tuple-element.4) | data formatting | bytes 16777216
  76.2 0.0 copy-done
  76.2 0.6 copy.8
Async XLA Ops:
  67.7 8.5 %copy-start = (f32[32,32]{1,0:T(8,128)S(1)}, f32[32,32]{1,0:T(8,128)}, u32[]{:S(2)}) copy-start(f32[32,32]{1,0:T(8,128)} %get-tuple-element.5) | copy-start | bytes 12292

commit v2 on v1

--- a/solution.py
+++ b/solution.py
@@ -31,8 +31,8 @@
     return high, (x - high.astype(F32)).astype(BF16)
 
 
-def kernel(n, field, occ, duals, out, duals_out, u, v0, v1, parts, mask, keep, acc, mix, shift,
-           gsend, gbuf, in_sem, out_sem, h_send, h_recv, m_send, m_recv, g_send, g_recv):
+def kernel(n, field, occ, duals, u, duals_out, v0, v1, parts, mask, keep, acc, mix, shift,
+           gsend, gbuf, in_sem, h_send, h_recv, m_send, m_recv, g_send, g_recv):
     me = lax.axis_index("gx")
     rows, channels, depth, across = u.shape
     wide = channels * S8
@@ -301,12 +301,8 @@
     beta = mixing(gram_end(1), beta)
     duals_out[...] = beta
 
-    def store(x):
-        return pltpu.make_async_copy(u.at[x], out.at[:, x], out_sem.at[x])
-
     def second(x, c):
         advance_row(v1, x, write_last)
-        store(x).start()
         return c
 
     lax.fori_loop(1, rows - 1, second, 0)
@@ -335,8 +331,6 @@
     @pl.when(me < n - 1)
     def _():
         w_r.wait_send()
-
-    lax.fori_loop(0, rows, lambda x, c: (store(x).wait(), c)[1], 0)
 
 
 def per_device(field, occupancy, duals):
@@ -345,13 +339,12 @@
     wide = channels * S8
     vmem = pl.BlockSpec(memory_space=pltpu.VMEM)
     dma = pltpu.SemaphoreType.DMA
-    return pl.pallas_call(
+    held, beta = pl.pallas_call(
         functools.partial(kernel, n),
-        out_shape=(jax.ShapeDtypeStruct(field.shape, F32), jax.ShapeDtypeStruct(duals.shape, F32)),
+        out_shape=(pltpu.VMEM((rows, channels, depth, across), F32), jax.ShapeDtypeStruct(duals.shape, F32)),
         in_specs=[pl.BlockSpec(memory_space=pl.ANY), vmem, vmem],
-        out_specs=(pl.BlockSpec(memory_space=pl.ANY), vmem),
+        out_specs=(vmem, vmem),
         scratch_shapes=[
-            pltpu.VMEM((rows, channels, depth, across), F32),
             pltpu.VMEM((rows + 2, channels, depth, across), F32),
             pltpu.VMEM((rows + 2, channels, depth, across), F32),
             pltpu.VMEM((rows, 2 * wide, depth // S8 * across), BF16),
@@ -362,11 +355,13 @@
             pltpu.VMEM((2 * across, across), BF16),
             pltpu.VMEM((2, S8, across), F32),
             pltpu.VMEM((2, n, S8, across), F32),
-            dma((rows,)), dma((rows,)), dma((6,)), dma((6,)), dma((2,)), dma((2,)), dma((2, n)), dma((2, n)),
+            dma((rows,)), dma((6,)), dma((6,)), dma((2,)), dma((2,)), dma((2, n)), dma((2, n)),
         ],
         compiler_params=pltpu.CompilerParams(
-            collective_id=0, has_side_effects=True, vmem_limit_bytes=56 * 1024 * 1024),
+            collective_id=0, has_side_effects=True, vmem_limit_bytes=40 * 1024 * 1024),
     )(field, occupancy, duals)
+    result = jnp.transpose(held, (1, 0, 2, 3))
+    return result, beta
 
 
 def solution(mesh):

time: 77 us -> 72.7 us (0.944)
  Pallas kernels: 67.1 us -> 64.5 us
  local copies, waits for them, and re-layouts: 9.06 us -> 7.33 us
    pallas_call x1, Pallas kernels: 67.1 us -> 64.5 us  [per_device(): pl.pallas_call(functools.partial(kernel, n), out_shape=(pltpu.VMEM((rows,...]
    unnamed x4 -> x6, local copies, waits for them, and re-layouts: 9.06 us -> 7.33 us
where the time goes in v2:
time: 72.7 us; the launch traced here: 72.5 us
  Pallas kernels  64.5 us (89%)
  local copies, waits for them, and re-layouts  7.33 us (10%)
    pallas_call x1, Pallas kernels, per_device(): pl.pallas_call(functools.partial(kernel, n), out_shape=(pltpu.VMEM((rows,...  64.5 us
    unnamed x6, local copies, waits for them, and re-layouts  7.33 us

profile of v2, /device:TPU:11, one launch (start us, length us, event | category | flops | bytes accessed | tf_op | source)
XLA Modules:
  0.0 72.5 jit_solution(3023406084764991290)
XLA Ops:
  0.6 0.0 copy-start
  0.6 0.9 %copy-done = s32[8,64,128]{2,1,0:T(8,128)S(1)} copy-done((s32[8,64,128]{2,1,0:T(8,128)S(1)}, s32[8,64,128]{2,1,0:T(8,128)}, u32[]{:S(2)}) %copy-start) | copy-done | bytes 262168
  1.6 0.0 copy-start.1
  1.6 0.7 copy-done.1
  2.3 64.5 %shard_map.50 = (f32[8,32,64,128]{3,2,1,0:T(8,128)S(1)}, f32[32,32]{1,0:T(8,128)S(1)}) custom-call(f32[32,8,64,128]{3,2,1,0:T(8,128)} %field.1, s32[8,64,128]{2,1,0:T(8,128)S(1)} %copy-done, f32[32,32]{1,0:T(8,128)S(1)} %copy-done.1), custom_call_target="tpu_custom_call" | custom-call | tf_op jit(solution)/shard_map/pallas_call | solution.py:342
  66.8 5.1 %copy.5 = f32[32,8,64,128]{3,2,1,0:T(8,128)} copy(f32[32,8,64,128]{3,2,0,1:T(8,128)S(1)} %bitcast.1) | data formatting | bytes 16777216
  71.9 0.6 copy.7
Async XLA Ops:
  0.6 1.0 %copy-start = (s32[8,64,128]{2,1,0:T(8,128)S(1)}, s32[8,64,128]{2,1,0:T(8,128)}, u32[]{:S(2)}) copy-start(s32[8,64,128]{2,1,0:T(8,128)} %occ.1) | copy-start | bytes 786436
  1.6 0.7 copy-start.1

commit v3 on v2

--- a/solution.py
+++ b/solution.py
@@ -81,7 +81,7 @@
 
     mask_l = to_left(mask.at[1], mask.at[last], m_send.at[0], m_recv.at[0])
     mask_r = to_right(mask.at[rows], mask.at[0], m_send.at[1], m_recv.at[1])
-    cut = channels * 3 // 8
+    cut = channels * 2 // 8
     pieces = (pl.ds(0, cut), pl.ds(cut, channels - cut))
     u_l = [to_left(u.at[0, p], v0.at[last, p], h_send.at[i], h_recv.at[i]) for i, p in enumerate(pieces)]
     u_r = [to_right(u.at[rows - 1, p], v0.at[0, p], h_send.at[2 + i], h_recv.at[2 + i]) for i, p in enumerate(pieces)]

time: 72.7 us -> 71.3 us (0.981)
  Pallas kernels: 64.5 us -> 63.1 us
    pallas_call x1, Pallas kernels: 64.5 us -> 63.1 us  [per_device(): pl.pallas_call(functools.partial(kernel, n), out_shape=(pltpu.VMEM((rows,...]
where the time goes in v3:
time: 71.3 us; the launch traced here: 71.1 us
  Pallas kernels  63.1 us (88%)
  local copies, waits for them, and re-layouts  7.33 us (10%)
    pallas_call x1, Pallas kernels, per_device(): pl.pallas_call(functools.partial(kernel, n), out_shape=(pltpu.VMEM((rows,...  63.1 us
    unnamed x6, local copies, waits for them, and re-layouts  7.33 us

profile of v3, /device:TPU:11, one launch (start us, length us, event | category | flops | bytes accessed | tf_op | source)
XLA Modules:
  0.0 71.1 jit_solution(1799382933296249116)
XLA Ops:
  0.6 0.0 copy-start
  0.6 0.9 %copy-done = s32[8,64,128]{2,1,0:T(8,128)S(1)} copy-done((s32[8,64,128]{2,1,0:T(8,128)S(1)}, s32[8,64,128]{2,1,0:T(8,128)}, u32[]{:S(2)}) %copy-start) | copy-done | bytes 262168
  1.6 0.0 copy-start.1
  1.6 0.7 %copy-done.1 = f32[32,32]{1,0:T(8,128)S(1)} copy-done((f32[32,32]{1,0:T(8,128)S(1)}, f32[32,32]{1,0:T(8,128)}, u32[]{:S(2)}) %copy-start.1) | copy-done | bytes 4120
  2.3 63.1 %shard_map.50 = (f32[8,32,64,128]{3,2,1,0:T(8,128)S(1)}, f32[32,32]{1,0:T(8,128)S(1)}) custom-call(f32[32,8,64,128]{3,2,1,0:T(8,128)} %field.1, s32[8,64,128]{2,1,0:T(8,128)S(1)} %copy-done, f32[32,32]{1,0:T(8,128)S(1)} %copy-done.1), custom_call_target="tpu_custom_call" | custom-call | tf_op jit(solution)/shard_map/pallas_call | solution.py:342
  65.4 5.1 %copy.5 = f32[32,8,64,128]{3,2,1,0:T(8,128)} copy(f32[32,8,64,128]{3,2,0,1:T(8,128)S(1)} %bitcast.1) | data formatting | bytes 16777216
  70.5 0.6 copy.7
Async XLA Ops:
  0.6 1.0 %copy-start = (s32[8,64,128]{2,1,0:T(8,128)S(1)}, s32[8,64,128]{2,1,0:T(8,128)}, u32[]{:S(2)}) copy-start(s32[8,64,128]{2,1,0:T(8,128)} %occ.1) | copy-start | bytes 786436
  1.6 0.7 %copy-start.1 = (f32[32,32]{1,0:T(8,128)S(1)}, f32[32,32]{1,0:T(8,128)}, u32[]{:S(2)}) copy-start(f32[32,32]{1,0:T(8,128)} %duals.1) | copy-start | bytes 12292
